TPU v7x, 256 devices: a whole 4x4x8 slice. The times are simulated.
256 devices in a mesh: rows: 32 (over x, z), cols: 8 (over y, core).
Axes of the slice: x: 4, y: 4, z: 8, core: 2. Of those that a mesh axis runs over, the one named last changes fastest.
Arguments:
- integrals: bfloat16 [32, 16, 64, 24576], P(None, None, 'rows', 'cols'), may hold values from -6 to 6
- density: bfloat16 [2048, 2048], P('cols', 'rows'), may hold values from -0.1875 to 0.1875
- neighbours: int32 [32, 16], replicated, may hold values from 0 to 31, all different within a row
- live: int32 [32], replicated, may hold values from 2 to 16, as said below
- sizes: int32 [32], replicated, may hold values from 48 to 64, as said below
Outputs:
- contracted: bfloat16 [32, 16, 64, 24576], P('rows', None, None, 'cols')
Inputs may be any that keep to these rules, and one draw needn't show every extreme that they name: `neighbours`: each row names 16 different blocks; every block is named by some row. Some block has all 16 slots live. `sizes`: some block has 64 functions.
All inputs are finite; a program needn't handle non-finite values.
Results may differ from a plain program's by a relative error of at most 0.001.
Values may be sent and summed in bfloat16 or wider, within the bound.
A program may use at most 128 MiB of HBM per device.

v0:
```python
import functools

import jax
import jax.numpy as jnp
from jax import lax
from jax.experimental import pallas as pl
from jax.experimental.pallas import tpu as pltpu
from jax.sharding import PartitionSpec as P

BS = 64
NX, NZ, NC = 4, 8, 8
NR = NX * NZ
MESH = pl.DeviceIdType.MESH
CHUNKS = (4, 4, 6, 4, 2, 2, 1, 1)
FIRST = tuple(sum(CHUNKS[:i]) for i in range(len(CHUNKS)))
AHEAD = 4
READY = 3
MULTIPLY = {READY + 1: ((0, 1),), READY + 2: ((2,),), READY + 3: ((3, 4),), READY + 4: ((5,), (6, 7))}
CAPACITIES = (44, 46, 48, 50, 52, 54, 58, 64)


def exchange(capacity, x_ref, d_ref, table, neigh, live, sizes, y_ref, d1, mine, d2, sel, ready, stage, *rest):
    n = len(CHUNKS)
    x_in, z_send, z_recv, x_send = (rest[i * n:(i + 1) * n] for i in range(4))
    in_sem, out_sem, zss, zrs, zos, xss, xrs, xos, dzs, dzr, dxs, dxr, dys, dyr, dsem = rest[4 * n:]
    row = lax.axis_index("rows")
    col = lax.axis_index("cols")
    x, z = row // NZ, lax.rem(row, NZ)
    slots = neigh.shape[0]
    units = NX * slots
    wide = slots * BS

    def at(dx, dz):
        return lax.rem(x + dx, NX) * NZ + lax.rem(z + dz, NZ)

    def far_first(i):
        return 4 + (i // 2) * (1 - lax.rem(i, 2)) - ((i + 1) // 2) * lax.rem(i, 2)

    def load(c):
        return pltpu.make_async_copy(x_ref.at[:, pl.ds(FIRST[c], CHUNKS[c])], x_in[c], in_sem.at[c])

    def each(count, copy, act):
        @pl.loop(0, count)
        def _(i):
            act(copy(i))

    def start(cp):
        cp.start()

    def wait(cp):
        cp.wait()

    def z_copy(c, i):
        dz = far_first(i)
        return pltpu.make_async_remote_copy(
            src_ref=z_send[c].at[dz], dst_ref=z_recv[c].at[z], send_sem=zss.at[c, i], recv_sem=zrs.at[c, i],
            device_id=(at(0, dz), col), device_id_type=MESH)

    def z_own(c):
        return pltpu.make_async_copy(z_send[c].at[0], z_recv[c].at[z], zos.at[c])

    def landing(c):
        return ready.at[pl.ds(FIRST[c], CHUNKS[c]), :, pl.ds(pl.multiple_of(x * 16, 16), 16)]

    def x_copy(c, i):
        dx = i + 1
        return pltpu.make_async_remote_copy(
            src_ref=x_send[c].at[lax.rem(x + dx, NX)], dst_ref=landing(c), send_sem=xss.at[c, i], recv_sem=xrs.at[c, i],
            device_id=(at(dx, 0), col), device_id_type=MESH)

    def x_own(c):
        return pltpu.make_async_copy(x_send[c].at[x], landing(c), xos.at[c])

    def dz_copy(i):
        return pltpu.make_async_remote_copy(
            src_ref=d_ref, dst_ref=d1.at[row], send_sem=dzs.at[i], recv_sem=dzr.at[i],
            device_id=(at(0, i + 1), col), device_id_type=MESH)

    def dx_copy(i):
        here = d1.at[pl.ds(x * NZ, NZ)]
        return pltpu.make_async_remote_copy(
            src_ref=here, dst_ref=here, send_sem=dxs.at[i], recv_sem=dxr.at[i],
            device_id=(at(i + 1, 0), col), device_id_type=MESH)

    def dy_copy(i):
        return pltpu.make_async_remote_copy(
            src_ref=mine, dst_ref=d2.at[col], send_sem=dys.at[i], recv_sem=dyr.at[i],
            device_id=(row, lax.rem(col + i + 1, NC)), device_id_type=MESH)

    for c in range(n):
        load(c).start()
    own_d = pltpu.make_async_copy(d_ref, d1.at[row], dsem)
    own_d.start()

    barrier = pltpu.get_barrier_semaphore()
    for dz in range(1, NZ):
        pl.semaphore_signal(barrier, inc=1, device_id=(at(0, dz), col), device_id_type=MESH)
    for dx in range(1, NX):
        pl.semaphore_signal(barrier, inc=1, device_id=(at(dx, 0), col), device_id_type=MESH)
    for dc in range(1, NC):
        pl.semaphore_signal(barrier, inc=1, device_id=(row, lax.rem(col + dc, NC)), device_id_type=MESH)
    pl.semaphore_wait(barrier, NZ + NX + NC - 3)

    def pack(c):
        load(c).wait()

        @pl.loop(0, capacity)
        def _(s):
            for dz in range(NZ):
                z_send[c][dz, s] = x_in[c][table[lax.rem(z + dz, NZ), s]]

    def send_z(c):
        each(NZ - 1, functools.partial(z_copy, c), start)
        z_own(c).start()

    def unpack(c):
        @pl.loop(0, units)
        def _(p):
            place = table[NZ + z, p]
            for other in range(NZ):
                for j in range(CHUNKS[c]):
                    x_send[c][p // slots, j, lax.rem(p, slots), 2 * other:2 * other + 2, :] = z_recv[c][other, place, j]

    each(NZ - 1, dz_copy, start)
    for c in range(AHEAD):
        pack(c)
        send_z(c)
    own_d.wait()
    each(NZ - 1, dz_copy, wait)
    each(NX - 1, dx_copy, start)
    for c in range(AHEAD, n):
        pack(c)

    def limit_of(k):
        return jnp.where(k < live[row], sizes[neigh[k, row]], 0)

    def density_rows():
        each(NX - 1, dx_copy, wait)
        inner = lax.broadcasted_iota(jnp.int32, (BS, 256), 0)

        @pl.loop(0, slots)
        def _(k):
            mine[pl.ds(pl.multiple_of(k * BS, BS), BS), :] = jnp.where(
                inner < limit_of(k), d1[neigh[k, row]], jnp.zeros((), jnp.bfloat16))

        each(NC - 1, dy_copy, start)
        d2[col] = mine[...]

    def density_columns():
        each(NC - 1, dy_copy, wait)
        index = lax.broadcasted_iota(jnp.int32, (256, 128), 0)
        lane = lax.broadcasted_iota(jnp.int32, (256, 128), 1)

        @pl.loop(0, slots // 2)
        def _(pair):
            picks = []
            for h in range(2):
                other = neigh[2 * pair + h, row]
                here = (lane >= h * BS) & (lane < h * BS + limit_of(2 * pair + h))
                hit = here & (index == lax.rem(other, 4) * BS + lane - h * BS)
                picks.append((other // 4, jnp.where(hit, 1.0, 0.0).astype(jnp.bfloat16)))

            @pl.loop(0, wide // 256)
            def _(part):
                rows_here = pl.ds(pl.multiple_of(part * 256, 256), 256)
                total = sum(jnp.dot(d2[c, rows_here, :], pick, preferred_element_type=jnp.float32) for c, pick in picks)
                sel[rows_here, pl.ds(pl.multiple_of(pair * 128, 128), 128)] = total.astype(jnp.bfloat16)

    keep = lax.rem(lax.broadcasted_iota(jnp.int32, (1, 256), 1), BS) < sizes[row]

    def multiply(chunks):
        for c in chunks:
            each(NX - 1, functools.partial(x_copy, c), wait)
            x_own(c).wait()

        first, last = FIRST[chunks[0]], FIRST[chunks[-1]] + CHUNKS[chunks[-1]]

        @pl.loop(0, (last - first) // 2)
        def _(pair):
            t = first + 2 * pair
            right = jnp.concatenate([ready[t].reshape(wide, 128), ready[t + 1].reshape(wide, 128)], axis=1)

            @pl.loop(0, slots // 4)
            def _(part):
                left = sel[pl.ds(pl.multiple_of(part * 256, 256), 256), :]
                out = jnp.dot(left, right, preferred_element_type=jnp.float32)
                tile = jnp.where(keep, out, 0.0).astype(jnp.bfloat16)
                stage[pl.ds(part * 4, 4), :, pl.ds(pl.multiple_of(t * 128, 256), 256)] = tile.reshape(4, BS, 256)

        cp = pltpu.make_async_copy(
            stage.at[:, :, pl.ds(first * 128, (last - first) * 128)],
            y_ref.at[0, :, :, pl.ds(first * 128, (last - first) * 128)], out_sem.at[chunks[0]])
        cp.start()
        return cp

    stores = []
    for c in range(n):
        each(NZ - 1, functools.partial(z_copy, c), wait)
        z_own(c).wait()
        if c + AHEAD < n:
            send_z(c + AHEAD)
        unpack(c)
        each(NX - 1, functools.partial(x_copy, c), start)
        x_own(c).start()
        if c == 0:
            density_rows()
        if c == READY:
            density_columns()
        if c in MULTIPLY:
            stores += [multiply(chunks) for chunks in MULTIPLY[c]]
    for cp in stores:
        cp.wait()


def tables(live, slots):
    counts = live.reshape(NX, NZ)
    ends = [counts[0]]
    for i in range(1, NX):
        ends.append(ends[-1] + counts[i])
    starts = [jnp.zeros_like(ends[0])] + ends[:-1]
    place = jnp.arange(NX * slots, dtype=jnp.int32)[None, :]
    target = jnp.arange(NZ, dtype=jnp.int32)[:, None]
    unit = jnp.zeros((NZ, NX * slots), jnp.int32)
    back = jnp.zeros((NZ, NX * slots), jnp.int32)
    for i in range(NX):
        start, end = starts[i][:, None], ends[i][:, None]
        unit = jnp.where((place >= start) & (place < end), (i * NZ + target) * slots + place - start, unit)
        slot = jnp.minimum(place - i * slots, end - start - 1)
        back = jnp.where((place >= i * slots) & (place < (i + 1) * slots), start + jnp.maximum(slot, 0), back)
    return jnp.concatenate([unit, back], axis=0), jnp.max(ends[-1])


def shards(integrals, density, neighbours, live, sizes):
    blocks, slots, rows_each, width = integrals.shape
    lanes = width // 128
    view = integrals.reshape(blocks * slots, rows_each, lanes, 128).transpose(0, 2, 1, 3)
    dma = pltpu.SemaphoreType.DMA
    smem = pl.BlockSpec(memory_space=pltpu.SMEM)
    anywhere = pl.BlockSpec(memory_space=pl.ANY)
    vmem = pl.BlockSpec(memory_space=pltpu.VMEM)
    wide = slots * BS
    n = len(CHUNKS)
    table, most = tables(live, slots)

    def call(which, capacity, *operands):
        def buffers(*lead):
            return [pltpu.VMEM(lead + (q, rows_each, 128), jnp.bfloat16) for q in CHUNKS]

        return pl.pallas_call(
            functools.partial(exchange, capacity),
            out_shape=jax.ShapeDtypeStruct((1, slots, BS, width), jnp.bfloat16),
            in_specs=[anywhere, vmem, smem, smem, smem, smem],
            out_specs=anywhere,
            scratch_shapes=[
                pltpu.VMEM((NR, BS, 256), jnp.bfloat16),
                pltpu.VMEM((wide, 256), jnp.bfloat16),
                pltpu.VMEM((NC, wide, 256), jnp.bfloat16),
                pltpu.VMEM((wide, wide), jnp.bfloat16),
                pltpu.VMEM((lanes, slots, BS, 128), jnp.bfloat16),
                pltpu.VMEM((slots, BS, width), jnp.bfloat16),
                *buffers(blocks * slots), *buffers(NZ, capacity), *buffers(NZ, capacity),
                *[pltpu.VMEM((NX, q, slots, NZ * rows_each, 128), jnp.bfloat16) for q in CHUNKS],
                dma((n,)), dma((n,)),
                dma((n, NZ - 1)), dma((n, NZ - 1)), dma((n,)),
                dma((n, NX - 1)), dma((n, NX - 1)), dma((n,)),
                dma((NZ - 1,)), dma((NZ - 1,)),
                dma((NX - 1,)), dma((NX - 1,)),
                dma((NC - 1,)), dma((NC - 1,)),
                dma,
            ],
            compiler_params=pltpu.CompilerParams(
                collective_id=which, has_side_effects=True, vmem_limit_bytes=48 * 2**20),
            name="exchange",
        )(*operands)

    which = sum((most > capacity).astype(jnp.int32) for capacity in CAPACITIES[:-1])
    return lax.switch(
        which, [functools.partial(call, i, capacity) for i, capacity in enumerate(CAPACITIES)],
        view, density.T, table, neighbours.T, live, sizes)


def solution(mesh):
    return jax.shard_map(
        shards,
        mesh=mesh,
        in_specs=(P(None, None, "rows", "cols"), P("cols", "rows"), P(), P(), P()),
        out_specs=P("rows", None, None, "cols"),
        check_vma=False,
    )
```

profile of v0, /device:TPU:8, one launch (start us, length us, event | category | flops | bytes accessed | tf_op | source)
XLA Modules:
  0.0 151.7 jit_solution(17925136153549376484)
XLA Ops:
  0.1 1.5 fusion.4
  6.1 0.1 select_select_fusion.1
  6.2 142.8 %conditional.1 = (bf16[1,16,64,3072]{3,2,1,0:T(8,128)(2,1)S(1)}) conditional(s32[]{:T(128)} %clamp.3, (bf16[512,24,2,128]{3,2,1,0:T(2,128)(2,1)}, bf16[64,256]{1,0:T(8,128)(2,1)}, s32[16,64]{1,0:T(8,128)S(1)}, s32[16,32]{1,0:T(8,128)}, s32[32]{0:T(128)}, /*index=5*/s32[32]{0:T(128)}) %tuple.79, ...), branch_computations={%region_1.2_spmd, %region_2.3_spmd, %region_3.4_spmd, %region_4.5_... | conditional | bytes 8 | solution.py:277
  6.5 142.2 %exchange.13 = bf16[1,16,64,3072]{3,2,1,0:T(8,128)(2,1)S(1)} custom-call(bf16[512,24,2,128]{3,2,1,0:T(2,128)(2,1)} %get-tuple-element.140.x_ref, bf16[64,256]{1,0:T(8,128)(2,1)} %get-tuple-element.141.d_ref, s32[16,64]{1,0:T(8,128)S(1)} %get-tuple-element.142.table, s32[16,32]{1,0:T(8,128)} %get-tuple-element.143.neigh, s32[32]{0:T(128)} %get-tuple-element.144.live, ...), custom_call_target="tpu_custom_call" | custom-call | tf_op jit(solution)/shard_map/cond/branch_5_fun/exchange/pallas_call | solution.py:249
  149.0 2.7 %copy.31 = bf16[1,16,64,3072]{3,2,1,0:T(8,128)(2,1)} copy(bf16[1,16,64,3072]{3,2,1,0:T(8,128)(2,1)S(1)} %get-tuple-element.158) | data formatting | bytes 12582912
  (7 shorter events, 0.0 us)
where the time goes:
time: 152 us
  Pallas kernels  142 us (93%)
  between operations  4.59 us (3%)
  local copies, waits for them, and re-layouts  2.71 us (2%)
  other arithmetic  1.64 us (1%)
    pallas_call x1, Pallas kernels, call(): pl.pallas_call(functools.partial(exchange, capacity), out_shape=jax.Shape...  142 us

commit v1 on v0

--- a/solution.py
+++ b/solution.py
@@ -14,8 +14,8 @@
 CHUNKS = (4, 4, 6, 4, 2, 2, 1, 1)
 FIRST = tuple(sum(CHUNKS[:i]) for i in range(len(CHUNKS)))
 AHEAD = 4
-READY = 3
-MULTIPLY = {READY + 1: ((0, 1),), READY + 2: ((2,),), READY + 3: ((3, 4),), READY + 4: ((5,), (6, 7))}
+READY = 2
+MULTIPLY = {3: ((0, 1),), 4: ((2,),), 5: ((3,),), 7: ((4, 5), (6, 7))}
 CAPACITIES = (44, 46, 48, 50, 52, 54, 58, 64)
 
 
@@ -146,6 +146,8 @@
         each(NC - 1, dy_copy, start)
         d2[col] = mine[...]
 
+    density_rows()
+
     def density_columns():
         each(NC - 1, dy_copy, wait)
         index = lax.broadcasted_iota(jnp.int32, (256, 128), 0)
@@ -202,8 +204,6 @@
         unpack(c)
         each(NX - 1, functools.partial(x_copy, c), start)
         x_own(c).start()
-        if c == 0:
-            density_rows()
         if c == READY:
             density_columns()
         if c in MULTIPLY:
@@ -227,7 +227,8 @@
         unit = jnp.where((place >= start) & (place < end), (i * NZ + target) * slots + place - start, unit)
         slot = jnp.minimum(place - i * slots, end - start - 1)
         back = jnp.where((place >= i * slots) & (place < (i + 1) * slots), start + jnp.maximum(slot, 0), back)
-    return jnp.concatenate([unit, back], axis=0), jnp.max(ends[-1])
+    over = sum((ends[-1] > capacity).astype(jnp.int32) for capacity in CAPACITIES[:-1])
+    return jnp.concatenate([unit, back], axis=0), jnp.max(over)
 
 
 def shards(integrals, density, neighbours, live, sizes):
@@ -240,7 +241,7 @@
     vmem = pl.BlockSpec(memory_space=pltpu.VMEM)
     wide = slots * BS
     n = len(CHUNKS)
-    table, most = tables(live, slots)
+    table, which = tables(live, slots)
 
     def call(which, capacity, *operands):
         def buffers(*lead):
@@ -273,7 +274,6 @@
             name="exchange",
         )(*operands)
 
-    which = sum((most > capacity).astype(jnp.int32) for capacity in CAPACITIES[:-1])
     return lax.switch(
         which, [functools.partial(call, i, capacity) for i, capacity in enumerate(CAPACITIES)],
         view, density.T, table, neighbours.T, live, sizes)

time: 152 us -> 135 us (0.89); the launches traced: 152 us -> 133 us
  Pallas kernels: 142 us -> 127 us
  between operations: 4.59 us -> 0.7 us
    pallas_call x1, Pallas kernels: 142 us -> 127 us  [call(): pl.pallas_call(functools.partial(exchange, capacity), out_shape=jax.Shape...]
where the time goes in v1:
time: 135 us; the launch traced here: 133 us
  Pallas kernels  127 us (94%)
  local copies, waits for them, and re-layouts  2.71 us (2%)
  other arithmetic  1.65 us (1%)
    pallas_call x1, Pallas kernels, call(): pl.pallas_call(functools.partial(exchange, capacity), out_shape=jax.Shape...  127 us
    unnamed x1, local copies, waits for them, and re-layouts  2.71 us

profile of v1, /device:TPU:8, one launch (start us, length us, event | category | flops | bytes accessed | tf_op | source)
XLA Modules:
  0.0 132.9 jit_solution(9234771224727195632)
XLA Ops:
  0.1 1.5 %fusion.10 = (s32[8]{0:T(128)S(1)}, s32[8]{0:T(128)S(1)}, s32[8]{0:T(128)S(1)}, s32[8]{0:T(128)S(1)}, s32[8]{0:T(128)S(1)}, /*index=5*/s32[]{:T(128)}, s32[8]{0:T(128)S(1)}, s32[8]{0:T(128)S(1)}, s32[8]{0:T(128)S(1)}) fusion(s32[32]{0:T(128)} %param.16), kind=kLoop, calls=%fused_computation.45 | loop fusion | flops 223 | bytes 388 | tf_op jit(solution)/shard_map/slice | solution.py:217
  2.2 0.1 select_select_fusion.1
  2.3 127.8 %conditional.1 = (bf16[1,16,64,3072]{3,2,1,0:T(8,128)(2,1)S(1)}) conditional(s32[]{:T(128)} %clamp.3, (bf16[512,24,2,128]{3,2,1,0:T(2,128)(2,1)}, bf16[64,256]{1,0:T(8,128)(2,1)}, s32[16,64]{1,0:T(8,128)S(1)}, s32[16,32]{1,0:T(8,128)}, s32[32]{0:T(128)}, /*index=5*/s32[32]{0:T(128)}) %tuple.79, ...), branch_computations={%region_1.2_spmd, %region_2.3_spmd, %region_3.4_spmd, %region_4.5_... | conditional | bytes 8 | solution.py:277
  2.4 127.2 %exchange.9 = bf16[1,16,64,3072]{3,2,1,0:T(8,128)(2,1)S(1)} custom-call(bf16[512,24,2,128]{3,2,1,0:T(2,128)(2,1)} %get-tuple-element.116.x_ref, bf16[64,256]{1,0:T(8,128)(2,1)} %get-tuple-element.117.d_ref, s32[16,64]{1,0:T(8,128)S(1)} %get-tuple-element.118.table, s32[16,32]{1,0:T(8,128)} %get-tuple-element.119.neigh, s32[32]{0:T(128)} %get-tuple-element.120.live, ...), custom_call_target="tpu_custom_call" | custom-call | tf_op jit(solution)/shard_map/cond/branch_1_fun/exchange/pallas_call | solution.py:250
  130.2 2.7 %copy.31 = bf16[1,16,64,3072]{3,2,1,0:T(8,128)(2,1)} copy(bf16[1,16,64,3072]{3,2,1,0:T(8,128)(2,1)S(1)} %get-tuple-element.158) | data formatting | bytes 12582912
  (7 shorter events, 0.0 us)
